TPU v7x, 256 devices: a whole 4x4x8 slice. The times are simulated.
256 devices in a mesh: ctx: 64 (over z, x, core), head: 4 (over y).
Axes of the slice: x: 4, y: 4, z: 8, core: 2. Of those that a mesh axis runs over, the one named last changes fastest.
Arguments:
- queries: bfloat16 [16384, 2560], P('ctx', 'head'), may hold values from -5 to 5
- keys: bfloat16 [16384, 512], P('ctx', 'head'), may hold values from -4.5 to 4.5
- values: bfloat16 [16384, 512], P('ctx', 'head'), may hold values from -6 to 6
- token_types: int32 [16384], P('ctx'), may hold values 0 or 1
- type_bias: float32 [20, 2, 2], P('head'), may hold values from -2 to 2
- out_weight: bfloat16 [2560, 5120], P('head'), may hold values from -0.125 to 0.125
Outputs:
- mixed: bfloat16 [16384, 5120], P('ctx', 'head')
All inputs are finite; a program needn't handle non-finite values. No bound on the sum of `token_types` on one device may be relied on, other than what follows from the above.
Results may differ from a plain program's by a relative error of at most 0.013.
Values may be sent and summed in bfloat16 or wider, within the bound.
No kernel may reach another device: no remote copies, remote signals or barrier semaphores. Data moves between devices by JAX's collectives and lax.ppermute only.
A program may use at most 128 MiB of HBM per device.

v0:
```python
import math

import jax
import jax.numpy as jnp
from jax import lax
from jax.sharding import PartitionSpec as P

masked_fill = -1e30


def type_term(bias_block, query_kind, key_kind):
    base_term = bias_block[:, 0, 0]
    query_step = bias_block[:, 1, 0] - bias_block[:, 0, 0]
    key_step = bias_block[:, 0, 1] - bias_block[:, 0, 0]
    joint_step = (
        bias_block[:, 1, 1] - bias_block[:, 1, 0] - bias_block[:, 0, 1] + bias_block[:, 0, 0]
    )
    outer_kind = query_kind[:, None] * key_kind[None, :]
    return (
        base_term[:, None, None]
        + query_step[:, None, None] * query_kind[None, :, None]
        + key_step[:, None, None] * key_kind[None, None, :]
        + joint_step[:, None, None] * outer_kind[None]
    )


def attend(state, segment, key_piece, value_piece, key_kind, key_pos, type_bias, score_scale):
    running_max, running_sum, accumulated = state
    query_rows, query_kind, query_pos = segment
    scores = (
        jnp.einsum("qgd,kd->gqk", query_rows, key_piece, preferred_element_type=jnp.float32)
        * score_scale
    )
    scores = scores + type_term(type_bias, query_kind, key_kind)
    visible = key_pos[None, :] <= query_pos[:, None]
    scores = jnp.where(visible[None], scores, masked_fill)
    new_max = jnp.maximum(running_max, jnp.max(scores, axis=-1))
    weights = jnp.where(visible[None], jnp.exp(scores - new_max[..., None]), 0.0)
    new_sum = jnp.sum(weights, axis=-1)
    update = jnp.einsum(
        "gqk,kd->gqd", weights.astype(jnp.bfloat16), value_piece, preferred_element_type=jnp.float32
    )
    return (new_max, new_sum, update)


def shards(queries, keys, values, token_types, type_bias, out_weight):
    ctx_index = lax.axis_index("ctx")
    rows = queries.shape[0]
    half_rows = rows // 2
    heads_local = type_bias.shape[0]
    head_width = keys.shape[1]
    score_scale = 1.0 / math.sqrt(head_width)
    first_positions = ctx_index * rows + jnp.arange(half_rows, dtype=jnp.int32)
    later_queries = queries[half_rows:]
    later_types = token_types[half_rows:]
    later_positions = ctx_index * rows + half_rows + jnp.arange(half_rows, dtype=jnp.int32)
    segments = (
        (
            queries[:half_rows].reshape(half_rows, heads_local, head_width),
            token_types[:half_rows].astype(jnp.float32),
            first_positions,
        ),
        (
            later_queries.reshape(half_rows, heads_local, head_width),
            later_types.astype(jnp.float32),
            later_positions,
        ),
    )

    def blank_state():
        return (
            jnp.full((heads_local, half_rows), masked_fill, jnp.float32),
            jnp.zeros((heads_local, half_rows), jnp.float32),
            jnp.zeros((heads_local, half_rows, head_width), jnp.float32),
        )

    carry = (blank_state(), blank_state())
    start = jnp.int32(0)
    key_piece = lax.all_gather(keys, "ctx", axis=0, tiled=True)
    value_piece = lax.all_gather(values, "ctx", axis=0, tiled=True)
    type_piece = lax.all_gather(token_types, "ctx", axis=0, tiled=True)
    piece_rows = key_piece.shape[0]
    key_pos = jnp.arange(piece_rows, dtype=jnp.int32)
    key_kind = type_piece.astype(jnp.float32)
    updated = []
    for state, segment in zip(carry, segments):

        def take(old_state, segment=segment):
            return attend(
                old_state,
                segment,
                key_piece,
                value_piece,
                key_kind,
                key_pos,
                type_bias,
                score_scale,
            )

        def leave(old_state):
            return old_state

        updated.append(lax.cond(start <= segment[2][-1], take, leave, state))
    final_states = tuple(updated)
    finished = []
    for running_max, running_sum, accumulated in final_states:
        normed = accumulated / running_sum[..., None]
        finished.append(
            jnp.transpose(normed, (1, 0, 2))
            .reshape(half_rows, heads_local * head_width)
            .astype(jnp.bfloat16)
        )
    lower_rows, upper_rows = finished
    attended = jnp.concatenate([lower_rows, upper_rows], axis=0)
    partial_out = jnp.dot(attended, out_weight, preferred_element_type=jnp.float32)
    return lax.psum_scatter(
        partial_out.astype(jnp.bfloat16), "head", scatter_dimension=1, tiled=True
    )


def solution(mesh):
    in_specs = (
        P("ctx", "head"),
        P("ctx", "head"),
        P("ctx", "head"),
        P("ctx"),
        P("head", None, None),
        P("head", None),
    )
    out_specs = P("ctx", "head")
    return jax.shard_map(shards, mesh=mesh, in_specs=in_specs, out_specs=out_specs, check_vma=False)
```

profile of v0, /device:TPU:224, one launch (start us, length us, event | category | flops | bytes accessed | tf_op | source)
XLA Modules:
  0.0 340.5 jit_solution(12278691069794935274)
XLA Ops:
  6.5 0.7 all-gather.4.cloned.1.call-update
  7.3 0.7 all-gather.6.cloned.1.call-update
  9.3 0.8 slice_convert_fusion.1
  11.3 43.2 %all-gather = s32[64,1,256]{2,1,0:T(1,128)S(1)} all-gather(s32[1,1,256]{2,1,0:T(1,128)} %bitcast.61), channel_id=1, replica_groups=mesh['ctx'=64,'head'=4] {'ctx'}, dimensions={0}, use_global_device_ids=true | all-gather | bytes 66560 | tf_op jit(solution)/shard_map/all_gather | solution.py:81
  54.6 33.6 %all-gather.4.cloned.1.call-done = bf16[16384,128]{1,0:T(8,128)(2,1)} async-done(((bf16[256,128]{1,0:T(8,128)(2,1)}), bf16[16384,128]{1,0:T(8,128)(2,1)}) %all-gather.4.cloned.1.call-update) | async-done | bytes 4194320 | tf_op jit(solution)/shard_map/all_gather | solution.py:79
  88.2 79.1 %all-gather.6.cloned.1.call-done = bf16[16384,128]{1,0:T(8,128)(2,1)} async-done(((bf16[256,128]{1,0:T(8,128)(2,1)}), bf16[16384,128]{1,0:T(8,128)(2,1)}) %all-gather.6.cloned.1.call-update) | async-done | bytes 4194320 | tf_op jit(solution)/shard_map/all_gather | solution.py:80
  167.3 62.2 %conditional.2 = (f32[5,128]{1,0:T(8,128)S(1)}, f32[5,128,128]{1,2,0:T(8,128)S(1)}) conditional(s32[]{:T(128)} %bitcast.16, () %tuple.21, (s32[16384]{0:T(1024)S(1)}, s32[128]{0:T(128)S(1)}, bf16[256,640]{1,0:T(8,128)(2,1)}, bf16[16384,128]{1,0:T(8,128)(2,1)}, f32[5,2,2]{0,2,1:T(2,128)}, /*index=5*/f32[128]{0:T(128)S(1)}, f32[16384]{0:T(1024)S(1)}, ...), branch_computations={%region_0.0_spmd, %region_1.4_spmd} | conditional | flops 5509301248 | bytes 178509584 | solution.py:103
  167.3 0.8 slice_bitcast_fusion
  168.1 1.1 copy.21
  169.4 7.4 %broadcast_compare_fusion = pred[128,16384]{0,1:T(8,128)(4,1)S(1)} fusion(s32[128]{0:T(128)S(1)} %get-tuple-element.42, s32[16384]{0:T(1024)S(1)} %get-tuple-element.41), kind=kLoop, calls=%fused_computation.10 | loop fusion | flops 2097152 | bytes 2163200 | tf_op jit(solution)/shard_map/cond/branch_1_fun/le | solution.py:35
  176.8 2.3 broadcast_multiply_fusion
  179.1 17.5 %fusion.22 = (f32[5,128]{1,0:T(8,128)S(1)}, f32[5,128,16384]{1,2,0:T(8,128)}) fusion(f32[128,16384]{0,1:T(8,128)S(1)} %broadcast_multiply_fusion, f32[5]{0:T(128)S(1)} %get-tuple-element.102, f32[5,16384]{1,0:T(8,128)S(1)} %broadcast_multiply_fusion.1, f32[5,128]{1,0:T(8,128)S(1)} %multiply_add_fusion, bf16[128,5,128]{0,2,1:T(8,128)(2,1)S(1)} %bitcast.59, ...), kind=kOutput, calls=%fused_computation.49 | convolution fusion | flops 2757754368 | bytes 57119764 | tf_op jit(solution)/shard_map/cond/branch_1_fun/qgd,kd->gqk/dot_general | solution.py:31
  196.6 15.9 %fusion.3 = f32[5,128,128]{1,2,0:T(8,128)S(1)} fusion(f32[5,128,16384]{1,2,0:T(8,128)} %get-tuple-element.104, f32[5,128]{1,0:T(8,128)S(1)} %broadcast_maximum_fusion, pred[128,16384]{0,1:T(8,128)(4,1)S(1)} %broadcast_compare_fusion, bf16[16384,128]{1,0:T(8,128)(2,1)S(1)} %copy-done), kind=kOutput, calls=%fused_computation.5 | convolution fusion | flops 2715811840 | bytes 48564736 | tf_op jit(solution)/shard_map/cond | solution.py:103
  212.5 17.0 %fusion.2 = f32[5,128]{1,0:T(8,128)S(1)} fusion(f32[5,128,16384]{1,2,0:T(8,128)} %get-tuple-element.104, f32[5,128]{1,0:T(8,128)S(1)} %broadcast_maximum_fusion, pred[128,16384]{0,1:T(8,128)(4,1)S(1)} %broadcast_compare_fusion), kind=kLoop, calls=%fused_computation.4 | loop fusion | flops 31456640 | bytes 44045312 | tf_op jit(solution)/shard_map/cond/branch_1_fun/reduce_sum | solution.py:39
  229.5 62.4 %conditional.3 = (f32[5,128]{1,0:T(8,128)S(1)}, f32[5,128,128]{1,2,0:T(8,128)S(1)}) conditional(s32[]{:T(128)} %bitcast.21, () %tuple.23, (s32[16384]{0:T(1024)S(1)}, s32[128]{0:T(128)S(1)}, bf16[256,640]{1,0:T(8,128)(2,1)}, bf16[16384,128]{1,0:T(8,128)(2,1)}, f32[5,2,2]{0,2,1:T(2,128)}, /*index=5*/f32[128]{0:T(128)S(1)}, f32[16384]{0:T(1024)S(1)}, ...), branch_computations={%region_4.5_spmd, %region_5.8_spmd} | conditional | flops 5509301248 | bytes 178509584 | solution.py:103
  229.7 0.8 slice_bitcast_fusion.1
  230.6 1.1 copy.23
  231.9 7.4 %broadcast_compare_fusion.1 = pred[128,16384]{0,1:T(8,128)(4,1)S(1)} fusion(s32[128]{0:T(128)S(1)} %get-tuple-element.50, s32[16384]{0:T(1024)S(1)} %get-tuple-element.49), kind=kLoop, calls=%fused_computation.29 | loop fusion | flops 2097152 | bytes 2163200 | tf_op jit(solution)/shard_map/cond/branch_1_fun/le | solution.py:35
  239.3 2.3 broadcast_multiply_fusion.2
  241.6 17.5 %fusion.23 = (f32[5,128]{1,0:T(8,128)S(1)}, f32[5,128,16384]{1,2,0:T(8,128)}) fusion(f32[128,16384]{0,1:T(8,128)S(1)} %broadcast_multiply_fusion.2, f32[5]{0:T(128)S(1)} %get-tuple-element.108, f32[5,16384]{1,0:T(8,128)S(1)} %broadcast_multiply_fusion.3, f32[5,128]{1,0:T(8,128)S(1)} %multiply_add_fusion.1, bf16[128,5,128]{0,2,1:T(8,128)(2,1)S(1)} %bitcast.60, ...), kind=kOutput, calls=%fused_computation.50 | convolution fusion | flops 2757754368 | bytes 57119764 | tf_op jit(solution)/shard_map/cond/branch_1_fun/qgd,kd->gqk/dot_general | solution.py:31
  259.1 15.8 %fusion.12 = f32[5,128,128]{1,2,0:T(8,128)S(1)} fusion(f32[5,128,16384]{1,2,0:T(8,128)} %get-tuple-element.110, f32[5,128]{1,0:T(8,128)S(1)} %broadcast_maximum_fusion.1, pred[128,16384]{0,1:T(8,128)(4,1)S(1)} %broadcast_compare_fusion.1, bf16[16384,128]{1,0:T(8,128)(2,1)S(1)} %copy-done.1), kind=kOutput, calls=%fused_computation.24 | convolution fusion | flops 2715811840 | bytes 48564736 | tf_op jit(solution)/shard_map/cond | solution.py:103
  274.9 17.0 %fusion.11 = f32[5,128]{1,0:T(8,128)S(1)} fusion(f32[5,128,16384]{1,2,0:T(8,128)} %get-tuple-element.110, f32[5,128]{1,0:T(8,128)S(1)} %broadcast_maximum_fusion.1, pred[128,16384]{0,1:T(8,128)(4,1)S(1)} %broadcast_compare_fusion.1), kind=kLoop, calls=%fused_computation.23 | loop fusion | flops 31456640 | bytes 44045312 | tf_op jit(solution)/shard_map/cond/branch_1_fun/reduce_sum | solution.py:39
  291.9 6.6 %convolution_convert_fusion = bf16[256,5120]{1,0:T(8,128)(2,1)} fusion(bf16[640,5120]{1,0:T(8,128)(2,1)} %param.15, bf16[128,640]{0,1:T(8,128)(2,1)S(1)} %bitcast.58, bf16[128,640]{0,1:T(8,128)(2,1)S(1)} %bitcast.57), kind=kOutput, calls=%fused_computation.38 | convolution fusion | flops 1679687680 | bytes 9502720 | tf_op jit(solution)/shard_map/dot_general | solution.py:115
  298.6 35.4 %reduce-scatter.2.cloned.1.call-done = bf16[256,1280]{1,0:T(8,128)(2,1)} async-done(((bf16[256,5120]{1,0:T(8,128)(2,1)}), bf16[256,1280]{1,0:T(8,128)(2,1)}) %reduce-scatter.2.cloned.1.call-update) | async-done | bytes 655376 | tf_op jit(solution)/shard_map/reduce_scatter | solution.py:116
  (24 shorter events, 1.8 us)
Async XLA Ops:
  6.5 81.7 %all-gather.4.cloned.1.call-start = ((), (), s32[]{:S(2)}) async-start(), calls=%async_computation.1 | async-start | bytes 4259840 | tf_op jit(solution)/shard_map/all_gather | solution.py:79
  7.3 160.0 %all-gather.6.cloned.1.call-start = ((), (), s32[]{:S(2)}) async-start(), calls=%async_computation.2 | async-start | bytes 4259840 | tf_op jit(solution)/shard_map/all_gather | solution.py:80
  8.0 325.9 %reduce-scatter.2.cloned.1.call-start = ((), (), s32[]{:S(2)}) async-start(), calls=%async_computation.3 | async-start | bytes 3276800 | tf_op jit(solution)/shard_map/reduce_scatter | solution.py:116
  179.1 17.5 %copy-start = (bf16[16384,128]{1,0:T(8,128)(2,1)S(1)}, bf16[16384,128]{1,0:T(8,128)(2,1)}, u32[]{:S(2)}) copy-start(bf16[16384,128]{1,0:T(8,128)(2,1)} %get-tuple-element.48) | copy-start | bytes 12582916 | tf_op jit(solution)/shard_map/cond
  241.6 17.5 %copy-start.1 = (bf16[16384,128]{1,0:T(8,128)(2,1)S(1)}, bf16[16384,128]{1,0:T(8,128)(2,1)}, u32[]{:S(2)}) copy-start(bf16[16384,128]{1,0:T(8,128)(2,1)} %get-tuple-element.56) | copy-start | bytes 12582916 | tf_op jit(solution)/shard_map/cond
Sparse Core Ops, SparseCore 0:
  10.1 78.0 all-gather.3
  91.0 76.2 all-gather.5
  298.7 35.1 reduce-scatter.1
where the time goes:
time: 344 us; the launch traced here: 340 us
  waiting for transfers between devices  149 us (43%)
  matrix products  73.3 us (21%)
  other arithmetic  56.2 us (16%)
  blocking collectives  43.2 us (13%)
  between operations  14.5 us (4%)
  local copies, waits for them, and re-layouts  3.49 us (1%)
    all_gather x1, waiting for transfers between devices, shards(): value_piece = lax.all_gather(values, 'ctx', axis=0, tiled=True)  79.1 us
    all_gather x1, blocking collectives, shards(): type_piece = lax.all_gather(token_types, 'ctx', axis=0, tiled=True)  43.2 us
    reduce_scatter x1, waiting for transfers between devices, shards(): lax.psum_scatter(partial_out.astype(jnp.bfloat16), 'head', scatter_dimens...  35.4 us
    dot_general x2, matrix products, attend(): jnp.einsum('qgd,kd->gqk', query_rows, key_piece, preferred_element_type=j...  34.9 us
    reduce_sum x2, other arithmetic, attend(): new_sum = jnp.sum(weights, axis=-1)  33.9 us
    all_gather x1, waiting for transfers between devices, shards(): key_piece = lax.all_gather(keys, 'ctx', axis=0, tiled=True)  33.6 us
    cond x2, matrix products, shards(): updated.append(lax.cond(start <= segment[2][-1], take, leave, state))  31.7 us
    le x2, other arithmetic, attend(): visible = key_pos[None, :] <= query_pos[:, None]  14.8 us
  transfers between devices with their start and end apart: 3, of which 3 were waited for; matrix products, arithmetic and copies ran while one was open for 1% of the time, Pallas kernels for 0%

commit v1 on v0

v1 whole, which is shorter than its diff:
```python
import functools
import math

import jax
import jax.numpy as jnp
from jax import lax
from jax.experimental import pallas as pl
from jax.experimental.pallas import tpu as pltpu
from jax.sharding import Mesh, PartitionSpec as P

f32 = jnp.float32
bf16 = jnp.bfloat16
HEAD = 128
EXTRA = 16
SUM_ROWS = 8
ACC_ROWS = HEAD + SUM_ROWS
STATE_ROWS = ACC_ROWS + 8
MASKED = -1e30
ROOM = 64.0
VMEM_LIMIT = 14 * 2**20
SMALL_LIMIT = 8 * 2**20
LOG2_SCALE = 1.4426950408889634 / math.sqrt(HEAD)


def stage_keys(blocks, first, keys_ref, values_ref):
    block = blocks[0].shape[0] - EXTRA
    row = lax.broadcasted_iota(jnp.int32, (EXTRA, HEAD), 0)
    col = lax.broadcasted_iota(jnp.int32, (EXTRA, HEAD), 1)
    spread = jnp.where((row < 2) & (col < 6) & (col % 2 == row), 1.0, 0.0).astype(bf16)
    for number, msg in enumerate(blocks):
        at = first + number * block
        keys_ref[at : at + block, :HEAD] = msg[:block, :HEAD]
        marks = lax.dot_general(
            msg[block:, :], spread, (((0,), (0,)), ((), ())), preferred_element_type=f32
        )
        keys_ref[at : at + block, HEAD:] = marks.astype(bf16)
        for part in range(block // HEAD):
            rows = slice(part * HEAD, (part + 1) * HEAD)
            cols = slice(at + part * HEAD, at + (part + 1) * HEAD)
            values_ref[:HEAD, cols] = msg[rows, HEAD:]
    total = len(blocks) * block
    values_ref[HEAD:, first : first + total] = jnp.ones((SUM_ROWS, total), bf16)


def blocks_of(refs):
    blocks = []
    for ref in refs:
        blocks += [ref] if len(ref.shape) == 2 else [ref.at[i] for i in range(ref.shape[0])]
    return blocks


def score(keys, queries):
    return lax.dot_general(keys, queries, (((1,), (1,)), ((), ())), preferred_element_type=f32)


def prepare_keys_kernel(keys_ref, values_ref, kind_ref, out_ref):
    block = keys_ref.shape[0]
    out_ref[:block, :HEAD] = keys_ref[...]
    for at in range(0, block, HEAD):
        turned = values_ref[at : at + HEAD, :].astype(f32).T
        out_ref[at : at + HEAD, HEAD:] = turned.astype(bf16)
    out_ref[block:, :] = type_marks(kind_ref)


def type_marks(kind_ref):
    kinds = jnp.broadcast_to(kind_ref[...].astype(f32), (EXTRA, kind_ref.shape[1]))
    row = lax.broadcasted_iota(jnp.int32, kinds.shape, 0)
    return jnp.where(row == 0, 1.0 - kinds, jnp.where(row == 1, kinds, 0.0)).astype(bf16)


def prepare_queries_kernel(bias_ref, query_ref, kind_ref, gate_ref, out_ref, token_ref):
    token_ref[0] = 0
    marks = type_marks(kind_ref)
    row = lax.broadcasted_iota(jnp.int32, (EXTRA, HEAD), 0)
    col = lax.broadcasted_iota(jnp.int32, (EXTRA, HEAD), 1)
    for head in range(out_ref.shape[0]):
        out_ref[head, :, :HEAD] = query_ref[:, head * HEAD : (head + 1) * HEAD]
        pairs = [bias_ref[4 * head + i] * math.sqrt(HEAD) for i in range(4)]
        first = jnp.where(col % 2 == 0, pairs[0], pairs[1])
        second = jnp.where(col % 2 == 0, pairs[2], pairs[3])
        table = jnp.where(row == 0, first, jnp.where(row == 1, second, 0.0))
        high = table.astype(bf16)
        rest = table - high.astype(f32)
        middle = rest.astype(bf16)
        low = (rest - middle.astype(f32)).astype(bf16)
        group = col // 2
        terms = jnp.where(
            group == 0,
            high.astype(f32),
            jnp.where(group == 1, middle.astype(f32), jnp.where(group == 2, low.astype(f32), 0.0)),
        ).astype(bf16)
        spread = lax.dot_general(
            marks, terms, (((0,), (0,)), ((), ())), preferred_element_type=f32
        )
        out_ref[head, :, HEAD:] = spread.astype(bf16)


def own_kernel(msgs, where_ref, mine_ref, other_ref, *refs):
    state_ref, token_ref, keys_ref, values_ref = refs[msgs:]
    blocks = blocks_of(refs[:msgs])
    slots = len(blocks)
    heads, block, _ = mine_ref.shape
    lanes = 2 * block
    stage_keys(blocks, 0, keys_ref, values_ref)
    token_ref[0] = where_ref[0] * 0
    lane = lax.broadcasted_iota(jnp.int32, (block, lanes), 1)
    query_pos = jnp.where(lane < block, where_ref[0] + lane, where_ref[1] + lane - block)
    ahead = lax.broadcasted_iota(jnp.int32, (block, lanes), 0) - query_pos

    def one_head(head, carry):
        queries = jnp.concatenate([mine_ref[head], other_ref[head]], axis=0)
        at = pl.ds(pl.multiple_of(head * lanes, HEAD), lanes)
        peak = jnp.full((1, lanes), MASKED, f32)
        parts = []
        for slot in range(slots):
            piece = score(keys_ref[slot * block : (slot + 1) * block, :], queries)
            piece = jnp.where(ahead <= -where_ref[2 + slot], piece, MASKED)
            peak = jnp.maximum(peak, jnp.max(piece, axis=0, keepdims=True))
            parts.append(piece)
        peak = jnp.where(peak > 0.5 * MASKED, peak, 0.0)
        shift = peak * LOG2_SCALE
        weights = jnp.concatenate(
            [jnp.exp2(part * LOG2_SCALE - shift).astype(bf16) for part in parts], axis=0
        )
        state_ref[:ACC_ROWS, at] = jnp.dot(values_ref[...], weights, preferred_element_type=f32)
        state_ref[ACC_ROWS:, at] = jnp.broadcast_to(peak, (8, lanes))
        return carry

    lax.fori_loop(0, heads, one_head, 0)


def add_keys(count, mine_ref, other_ref, keys_ref, values_ref, size, old_ref, state_ref):
    heads, block, _ = mine_ref.shape
    lanes = 2 * block
    state_ref[...] = old_ref[...]

    def queries_of(head):
        return jnp.concatenate([mine_ref[head], other_ref[head]], axis=0)

    def lanes_of(head):
        return pl.ds(pl.multiple_of(head * lanes, HEAD), lanes)

    def unit(step, worst):
        head, plane = step % heads, step // heads
        at = lanes_of(head)
        part = pl.ds(pl.multiple_of(plane * size, size), size)
        peak = old_ref[ACC_ROWS : ACC_ROWS + 1, at]
        mass = old_ref[HEAD : HEAD + 1, at]
        scores = score(keys_ref[part, :], queries_of(head))
        top = jnp.max(scores, axis=0, keepdims=True)
        weights = jnp.exp2(scores * LOG2_SCALE - peak * LOG2_SCALE).astype(bf16)
        state_ref[:ACC_ROWS, at] += jnp.dot(
            values_ref[:, part], weights, preferred_element_type=f32
        )
        rise = (top - peak) * LOG2_SCALE
        bad = (rise > ROOM) | ((mass <= 0.0) & (rise < -ROOM))
        return jnp.maximum(worst, jnp.where(bad, 1.0, 0.0))

    worst = lax.fori_loop(0, count, lambda p, w: functools.reduce(lambda w, h: unit(p * heads + h, w), range(heads), w), jnp.zeros((1, lanes), f32))

    @pl.when(jnp.max(worst) > 0.5)
    def _():
        state_ref[...] = old_ref[...]
        step_rows = 256
        chunks = size // step_rows

        def redo(step, carry):
            at = lanes_of(step % heads)
            part = pl.ds(pl.multiple_of((step // heads) * step_rows, step_rows), step_rows)
            peak = state_ref[ACC_ROWS : ACC_ROWS + 1, at]
            mass = state_ref[HEAD : HEAD + 1, at]
            scores = score(keys_ref[part, :], queries_of(step % heads))
            top = jnp.max(scores, axis=0, keepdims=True)
            fresh = jnp.where(mass > 0.0, jnp.maximum(peak, top), top)
            fade = jnp.where(mass > 0.0, jnp.exp2((peak - fresh) * LOG2_SCALE), 0.0)
            weights = jnp.exp2(scores * LOG2_SCALE - fresh * LOG2_SCALE).astype(bf16)
            update = jnp.dot(values_ref[:, part], weights, preferred_element_type=f32)
            state_ref[:ACC_ROWS, at] = state_ref[:ACC_ROWS, at] * fade + update
            state_ref[ACC_ROWS:, at] = jnp.broadcast_to(fresh, (8, lanes))
            return carry

        lax.fori_loop(0, heads * count * chunks, redo, 0)


def plane_kernel(plan, last, gates, count_ref, mine_ref, other_ref, *refs):
    msgs = 1 + max(index for plane in plan for index, _ in plane)
    old_ref = refs[msgs]
    if last:
        kept_ref, parcel_ref, state_ref, keys_ref, values_ref = refs[msgs + 1 + gates :]
    else:
        state_ref, token_ref, keys_ref, values_ref = refs[msgs + 1 + gates :]
    blocks = [blocks_of([ref]) for ref in refs[:msgs]]
    heads, block, _ = mine_ref.shape
    size = len(plan[0]) * block
    count = count_ref[0]
    for number, plane in enumerate(plan):

        @pl.when(count > number)
        def _(number=number, plane=plane):
            stage_keys([blocks[i][j] for i, j in plane], number * size, keys_ref, values_ref)

    add_keys(count, mine_ref, other_ref, keys_ref, values_ref, size, old_ref, state_ref)
    if not last:
        token_ref[0] = count * 0
        return
    for head in range(heads):
        finish(block, head, state_ref, kept_ref.at[head], parcel_ref.at[head])


def finish(block, head, state_ref, kept_ref, parcel_ref):
    at = slice(head * 2 * block, (head + 1) * 2 * block)
    mass = state_ref[HEAD : HEAD + 1, at]
    peak = state_ref[ACC_ROWS : ACC_ROWS + 1, at]
    full = mass > 0.0
    safe = jnp.where(full, mass, 1.0)
    level = jnp.where(full, peak * LOG2_SCALE + jnp.log2(safe), MASKED)
    mean = state_ref[:HEAD, at] * (1.0 / safe)
    kept_ref[:HEAD, :] = mean[:, :block]
    kept_ref[HEAD:, :] = jnp.broadcast_to(level[:, :block], (8, block))
    parcel_ref[:HEAD, :] = mean[:, block:].astype(bf16)
    whole = jnp.broadcast_to(level[:, block:], (EXTRA, block))
    high = whole.astype(bf16)
    rest = whole - high.astype(f32)
    middle = rest.astype(bf16)
    low = rest - middle.astype(f32)
    row = lax.broadcasted_iota(jnp.int32, whole.shape, 0)
    parcel_ref[HEAD:, :] = jnp.where(
        row == 0,
        high.astype(f32),
        jnp.where(row == 1, middle.astype(f32), jnp.where(row == 2, low, 0.0)),
    ).astype(bf16)


def merge_kernel(kept_ref, came_ref, low_ref, high_ref):
    half = low_ref.shape[0]
    for head in range(kept_ref.shape[0]):
        kept_level = kept_ref[head, HEAD : HEAD + 1, :]
        extra = came_ref[head, HEAD:, :].astype(f32)
        came_level = extra[0:1] + extra[1:2] + extra[2:3]
        top = jnp.maximum(kept_level, came_level)
        kept_part = jnp.exp2(kept_level - top)
        came_part = jnp.exp2(came_level - top)
        share = 1.0 / (kept_part + came_part)
        mixed = kept_ref[head, :HEAD, :] * (kept_part * share) + came_ref[head, :HEAD, :].astype(
            f32
        ) * (came_part * share)
        cols = slice(head * HEAD, (head + 1) * HEAD)
        low_ref[:, cols] = mixed[:, :half].T.astype(bf16)
        high_ref[:, cols] = mixed[:, half:].T.astype(bf16)


def tick_kernel(*refs):
    refs[-1][0] = 0


def after(*values):
    return pl.pallas_call(
        tick_kernel,
        in_specs=[pl.BlockSpec(memory_space=pl.ANY)] * len(values),
        out_specs=IN_SMEM,
        out_shape=jax.ShapeDtypeStruct((1,), jnp.int32),
        name="after",
    )(*values)[0]


def whole(value):
    return pl.BlockSpec(value.shape, lambda *_: (0,) * value.ndim)


IN_VMEM = pl.BlockSpec(memory_space=pltpu.VMEM)
IN_SMEM = pl.BlockSpec(memory_space=pltpu.SMEM)


def attend_own(where, mine, other, msgs):
    heads, block, depth = mine.shape
    lanes = 2 * block
    total = block * sum(1 if m.ndim == 2 else m.shape[0] for m in msgs)
    return pl.pallas_call(
        functools.partial(own_kernel, len(msgs)),
        in_specs=[IN_SMEM] + [IN_VMEM] * (2 + len(msgs)),
        out_specs=[IN_VMEM, IN_SMEM],
        scratch_shapes=[pltpu.VMEM((total, 2 * HEAD), bf16), pltpu.VMEM((ACC_ROWS, total), bf16)],
        out_shape=[
            jax.ShapeDtypeStruct((STATE_ROWS, heads * lanes), f32),
            jax.ShapeDtypeStruct((1,), jnp.int32),
        ],
        compiler_params=pltpu.CompilerParams(vmem_limit_bytes=VMEM_LIMIT),
        cost_estimate=pl.CostEstimate(
            flops=8 * heads * lanes * total * 256, bytes_accessed=2**20, transcendentals=0
        ),
        name="own_plane",
    )(where, mine, other, *msgs)


def attend_planes(count, mine, other, msgs, plan, state, last=False, gates=()):
    heads, block, depth = mine.shape
    lanes = 2 * block
    total = block * sum(len(plane) for plane in plan)
    scratch = [pltpu.VMEM((total, 2 * HEAD), bf16), pltpu.VMEM((ACC_ROWS, total), bf16)]
    if last:
        out_specs = [IN_VMEM, IN_VMEM]
        out_shape = [
            jax.ShapeDtypeStruct((heads, ACC_ROWS, block), f32),
            jax.ShapeDtypeStruct((heads, STATE_ROWS, block), bf16),
        ]
        scratch = [pltpu.VMEM((STATE_ROWS, heads * lanes), f32)] + scratch
    else:
        out_specs = [IN_VMEM, IN_SMEM]
        out_shape = [
            jax.ShapeDtypeStruct((STATE_ROWS, heads * lanes), f32),
            jax.ShapeDtypeStruct((1,), jnp.int32),
        ]
    return pl.pallas_call(
        functools.partial(plane_kernel, plan, last, len(gates)),
        in_specs=[IN_SMEM]
        + [IN_VMEM] * (3 + len(msgs))
        + [pl.BlockSpec(memory_space=pl.ANY)] * len(gates),
        out_specs=out_specs,
        scratch_shapes=scratch,
        out_shape=out_shape,
        compiler_params=pltpu.CompilerParams(vmem_limit_bytes=VMEM_LIMIT),
        cost_estimate=pl.CostEstimate(
            flops=6 * heads * lanes * total * 256, bytes_accessed=2**20, transcendentals=0
        ),
        name="last_planes" if last else "planes",
    )(count, mine, other, *msgs, state, *gates)


def joined(pair):
    return jnp.concatenate([pair[0][...], pair[1][...]], axis=0)


def near_kernel(core_ref, own, below, above, weights, out_ref):
    own_w, got_w, their_w = weights
    rows, width = below[0].shape[1], got_w.shape[1]
    out_ref[...] = jnp.dot(joined(own), own_w[...], preferred_element_type=f32)
    sides = jnp.concatenate([joined(below), joined(above)], axis=1)
    for side, weight in enumerate((got_w, their_w)):
        place = jnp.where(core_ref[0] == side, 0, width)
        at = pl.ds(pl.multiple_of(place, HEAD), width)
        out_ref[:, at] += jnp.dot(sides, weight[: 2 * rows, :], preferred_element_type=f32)


def far_kernel(core_ref, near_ref, pair, weights, out_ref):
    part = joined(pair)
    rows, width = part.shape[1], weights[0].shape[1]
    for side, weight in enumerate(weights):
        place = jnp.where(core_ref[0] == side, 0, width)
        at = pl.ds(pl.multiple_of(place, HEAD), width)
        more = jnp.dot(part, weight[2 * rows :, :], preferred_element_type=f32)
        out_ref[:, at] = (near_ref[:, at] + more).astype(bf16)


def project_near(core, own, below, above, weights):
    block, cols = 2 * own[0].shape[0], weights[0].shape[1]
    return pl.pallas_call(
        near_kernel,
        in_specs=[IN_SMEM, [IN_VMEM] * 2, [IN_VMEM] * 2, [IN_VMEM] * 2, [IN_VMEM] * 3],
        out_specs=IN_VMEM,
        out_shape=jax.ShapeDtypeStruct((block, cols), f32),
        compiler_params=pltpu.CompilerParams(vmem_limit_bytes=VMEM_LIMIT),
        name="project_near",
    )(core, list(own), below, above, weights)


def project_far(core, near, pair, weights):
    return pl.pallas_call(
        far_kernel,
        in_specs=[IN_SMEM, IN_VMEM, [IN_VMEM] * 2, [IN_VMEM] * 2],
        out_specs=IN_VMEM,
        out_shape=jax.ShapeDtypeStruct(near.shape, bf16),
        compiler_params=pltpu.CompilerParams(vmem_limit_bytes=VMEM_LIMIT),
        name="project_far",
    )(core, near, pair, weights)


def shift(value, axis, size, step):
    return lax.ppermute(value, axis, [(i, (i + step) % size) for i in range(size)])


def shards(sizes, queries, keys, values, token_types, type_bias, out_weight):
    nz, nx, nc, ny = sizes
    zi, xi, ci, yi = (lax.axis_index(a) for a in ("z", "x", "core", "head"))
    block = queries.shape[0]
    heads = type_bias.shape[0]
    kinds = token_types.reshape(1, block)

    message = pl.pallas_call(
        prepare_keys_kernel,
        out_shape=jax.ShapeDtypeStruct((block + EXTRA, 2 * HEAD), bf16),
        name="prepare_keys",
    )(keys, values, kinds)

    across = shift(message, "x", nx, 2)
    right = shift(message, "x", nx, 1)
    left = shift(message, "x", nx, -1)
    mine, token = pl.pallas_call(
        prepare_queries_kernel,
        in_specs=[IN_SMEM, IN_VMEM, IN_VMEM, pl.BlockSpec(memory_space=pl.ANY)],
        out_specs=[IN_VMEM, IN_SMEM],
        out_shape=[
            jax.ShapeDtypeStruct((heads, block, 2 * HEAD), bf16),
            jax.ShapeDtypeStruct((1,), jnp.int32),
        ],
        name="prepare_queries",
    )(type_bias.reshape(-1), queries, kinds, left)
    other = shift(mine, "core", nc, 1)
    plane = jnp.stack([message, right, across, left])

    forward, backward = [plane], [plane]
    for _ in range(3):
        forward.append(shift(forward[-1], "z", nz, 1))
        backward.append(shift(backward[-1], "z", nz, -1))
    far_parts = [forward[3][: nx // 2], backward[3][nx // 2 :]]
    far = [shift(far_parts[0], "z", nz, 1), shift(far_parts[1], "z", nz, -1)]

    rows_w, cols_w = out_weight.shape[0], out_weight.shape[1] // ny
    half = cols_w // nc

    def carve(step, gate, first=ci * half, cols=half):
        col = ((yi + step) % ny) * cols_w + first
        return lax.dynamic_slice(out_weight, (gate, col), (rows_w, cols))

    far_w = shift(carve(2, token[0]), "head", ny, 2)
    gate = after(plane)
    up_w = shift(carve(1, gate), "head", ny, 1)
    down_w = shift(carve(-1, gate), "head", ny, -1)

    chip = (zi * nx + xi) * nc
    homes = [((zi * nx + (xi - d) % nx) * nc + ci) * block for d in range(nx)]
    where = jnp.stack([(chip + ci) * block, (chip + 1 - ci) * block] + homes).astype(jnp.int32)
    state, token = attend_own(where, mine, other, [plane])
    planes = tuple(tuple((i, j) for j in range(nx)) for i in range(2))
    for step in (1, 2, 3):
        count = jnp.stack([jnp.where(zi >= nz - step, 2, jnp.where(zi >= step, 1, 0))])
        state, token = attend_planes(
            count.astype(jnp.int32),
            mine,
            other,
            [forward[step], backward[step]],
            planes,
            state,
            gates=far_parts if step == 3 else (),
        )
    got_w = jnp.concatenate([up_w, down_w, far_w]) + token[0].astype(bf16)
    their_w = shift(got_w, "core", nc, 1)
    own_w = carve(0, token[0], 0, cols_w)
    count = jnp.stack([jnp.where(zi >= nz // 2, 1, 0)]).astype(jnp.int32)
    kept, parcel = attend_planes(
        count, mine, other, far, (((0, 0), (0, 1), (1, 0), (1, 1)),), state, last=True
    )

    came = shift(parcel, "core", nc, 1)
    own = pl.pallas_call(
        merge_kernel,
        out_shape=[jax.ShapeDtypeStruct((block // 2, heads * HEAD), bf16)] * 2,
        compiler_params=pltpu.CompilerParams(vmem_limit_bytes=SMALL_LIMIT),
        name="merge",
    )(kept, came)

    below = [shift(own[0], "head", ny, 1), None]
    above = [None, shift(own[1], "head", ny, -1)]
    below[1] = shift(own[1], "head", ny, 1)
    above[0] = shift(own[0], "head", ny, -1)
    opposite = [shift(below[0], "head", ny, 1), shift(above[1], "head", ny, -1)]
    core = jnp.stack([ci]).astype(jnp.int32)
    near = project_near(core, own, below, above, [own_w, got_w, their_w])
    return project_far(core, near, opposite, [got_w, their_w])


def solution(mesh):
    nz, nx, nc, ny = 8, 4, 2, 4
    grid = Mesh(mesh.devices.reshape(nz, nx, nc, ny), ("z", "x", "core", "head"))
    ctx = ("z", "x", "core")
    in_specs = (
        P(ctx, "head"),
        P(ctx, "head"),
        P(ctx, "head"),
        P(ctx),
        P("head", None, None),
        P("head", None),
    )
    return jax.shard_map(
        functools.partial(shards, (nz, nx, nc, ny)),
        mesh=grid,
        in_specs=in_specs,
        out_specs=P(ctx, "head"),
        check_vma=False,
    )
```

time: 344 us -> 131 us (0.38)
  waiting for transfers between devices: 149 us -> 21.9 us
  matrix products: 73.3 us -> 0 us
  other arithmetic: 56.2 us -> 2.92 us
  starting transfers between devices: 0.08 us -> 48.9 us
  Pallas kernels: 0 us -> 43.9 us
  blocking collectives: 43.2 us -> 0 us
  between operations: 14.5 us -> 0.81 us
  local copies, waits for them, and re-layouts: 3.49 us -> 11.6 us
    all_gather x2 -> x0, waiting for transfers between devices: 113 us -> none  [the longest x1 79.1 us: shards(): value_piece = lax.all_gather(values, 'ctx', axis=0, tiled=True)]
    ppermute x0 -> x23, starting transfers between devices: none -> 48.9 us  [shift(): lax.ppermute(value, axis, [(i, (i + step) % size) for i in range(size)])]
    pallas_call x0 -> x10, Pallas kernels: none -> 43.9 us  [the longest x4 26.2 us: attend_planes(): pl.pallas_call(functools.partial(plane_kernel, plan, last, len(gates)), i...]
    all_gather x1 -> x0, blocking collectives: 43.2 us -> none  [shards(): type_piece = lax.all_gather(token_types, 'ctx', axis=0, tiled=True)]
    dot_general x3 -> x0, matrix products: 41.5 us -> none  [the longest x2 34.9 us: attend(): jnp.einsum('qgd,kd->gqk', query_rows, key_piece, preferred_element_type=j...]
    reduce_scatter x1 -> x0, waiting for transfers between devices: 35.4 us -> none  [shards(): lax.psum_scatter(partial_out.astype(jnp.bfloat16), 'head', scatter_dimens...]
    reduce_sum x2 -> x0, other arithmetic: 33.9 us -> none  [attend(): new_sum = jnp.sum(weights, axis=-1)]
    cond x2 -> x0, matrix products: 31.7 us -> none  [shards(): updated.append(lax.cond(start <= segment[2][-1], take, leave, state))]
  transfers between devices with their start and end apart: 3 -> 23, of which waited for: 3 -> 9; matrix products, arithmetic and copies ran while one was open for 1% -> 6% of each run, Pallas kernels for 0% -> 30%
where the time goes in v1:
time: 131 us; the launch traced here: 130 us
  starting transfers between devices  48.9 us (37%)
  Pallas kernels  43.9 us (34%)
  waiting for transfers between devices  21.9 us (17%)
  local copies, waits for them, and re-layouts  11.6 us (9%)
  other arithmetic  2.92 us (2%)
    ppermute x23, starting transfers between devices, shift(): lax.ppermute(value, axis, [(i, (i + step) % size) for i in range(size)])  48.9 us
    pallas_call x4, Pallas kernels, attend_planes(): pl.pallas_call(functools.partial(plane_kernel, plan, last, len(gates)), i...  26.2 us
    ppermute x23, waiting for transfers between devices, shift(): lax.ppermute(value, axis, [(i, (i + step) % size) for i in range(size)])  21.9 us
    pallas_call x1, Pallas kernels, attend_own(): pl.pallas_call(functools.partial(own_kernel, len(msgs)), in_specs=[IN_SME...  6.97 us
    unnamed x15, local copies, waits for them, and re-layouts  6.09 us
    dynamic_slice x2, local copies, waits for them, and re-layouts, carve(): return lax.dynamic_slice(out_weight, (gate, col), (rows_w, cols))  4.76 us
    pallas_call x1, Pallas kernels, project_near(): pl.pallas_call(near_kernel, in_specs=[IN_SMEM, [IN_VMEM] * 2, [IN_VMEM] *...  3.44 us
    pallas_call x1, Pallas kernels, project_far(): pl.pallas_call(far_kernel, in_specs=[IN_SMEM, IN_VMEM, [IN_VMEM] * 2, [IN...  3.31 us
  transfers between devices with their start and end apart: 23, of which 9 were waited for; matrix products, arithmetic and copies ran while one was open for 6% of the time, Pallas kernels for 30%

profile of v1, /device:TPU:224, one launch (start us, length us, event | category | flops | bytes accessed | tf_op | source)
XLA Modules:
  0.0 130.0 jit_solution(5213846727125902995)
XLA Ops:
  1.6 2.8 %collective-permute-start = (bf16[272,256]{1,0:T(8,128)(2,1)}, bf16[272,256]{1,0:T(8,128)(2,1)S(1)}, u32[]{:S(2)}, u32[]{:S(2)}) collective-permute-start(bf16[272,256]{1,0:T(8,128)(2,1)} %prepare_keys.1), channel_id=1, source_target_pairs={{0,24},{8,0},{16,8},{24,16},{1,25},{9,1},{17,9},{25,17},{2,26},{10... | collective-permute-start | bytes 417800 | tf_op jit(solution)/shard_map/ppermute | solution.py:378
  7.5 3.2 %collective-permute-done.gate_ref = bf16[272,256]{1,0:T(8,128)(2,1)S(1)} collective-permute-done((bf16[272,256]{1,0:T(8,128)(2,1)}, bf16[272,256]{1,0:T(8,128)(2,1)S(1)}, u32[]{:S(2)}, u32[]{:S(2)}) %collective-permute-start) | collective-permute-done | bytes 139296 | tf_op jit(solution)/shard_map/ppermute | solution.py:378
  11.3 2.1 %prepare_queries.1 = (bf16[5,256,256]{2,1,0:T(8,128)(2,1)}, s32[1]{0:T(128)}) custom-call(f32[20]{0:T(128)} %reshape.7.bias_ref, bf16[256,640]{1,0:T(8,128)(2,1)} %query_ref.1, s32[1,256]{1,0:T(1,128)} %bitcast.22, bf16[272,256]{1,0:T(8,128)(2,1)} %copy-done.6), custom_call_target="tpu_custom_call" | custom-call | tf_op jit(solution)/shard_map/prepare_queries/pallas_call | solution.py:397
  15.4 2.0 %collective-permute-start.8 = (bf16[4,272,256]{2,1,0:T(8,128)(2,1)S(1)}, bf16[4,272,256]{2,1,0:T(8,128)(2,1)S(1)}, u32[]{:S(2)}, u32[]{:S(2)}) collective-permute-start(bf16[4,272,256]{2,1,0:T(8,128)(2,1)S(1)} %pad_maximum_fusion.refs_0_), channel_id=1, source_target_pairs={{0,224},{32,0},{64,32},{96,64},{128,96},{160,128},{192,160},{224,1... | collective-permute-start | bytes 1671176 | tf_op jit(solution)/shard_map/ppermute | solution.py:378
  17.4 3.2 %constant_dynamic-slice_fusion.2 = (bf16[640,640]{1,0:T(8,128)(2,1)}, bf16[640,640]{1,0:T(8,128)(2,1)}, bf16[640,640]{1,0:T(8,128)(2,1)}) fusion(bf16[640,5120]{1,0:T(8,128)(2,1)} %param.11, s32[]{:T(128)S(6)} %select_n.88, s32[]{:T(128)S(6)} %select_n.92, s32[]{:T(128)S(6)} %select_n.90), kind=kLoop, calls=%fused_computation.4 | loop fusion | bytes 4915212 | tf_op jit(solution)/shard_map/dynamic_slice | solution.py:422
  20.6 3.2 %collective-permute-start.19 = (bf16[640,640]{1,0:T(8,128)(2,1)}, bf16[640,640]{1,0:T(8,128)(2,1)}, u32[]{:S(2)}, u32[]{:S(2)}) collective-permute-start(bf16[640,640]{1,0:T(8,128)(2,1)} %get-tuple-element.26), channel_id=1, source_target_pairs={{0,2},{1,3},{2,0},{3,1},{4,6},{5,7},{6,4},{7,5},{8,10},{9,11},{10,... | collective-permute-start | bytes 2457608 | tf_op jit(solution)/shard_map/ppermute | solution.py:378
  24.9 4.9 %collective-permute-done.4.refs_0_ = bf16[4,272,256]{2,1,0:T(8,128)(2,1)S(1)} collective-permute-done((bf16[4,272,256]{2,1,0:T(8,128)(2,1)S(1)}, bf16[4,272,256]{2,1,0:T(8,128)(2,1)S(1)}, u32[]{:S(2)}, u32[]{:S(2)}) %collective-permute-start.4) | collective-permute-done | bytes 557088 | tf_op jit(solution)/shard_map/ppermute | solution.py:378
  33.4 7.0 %own_plane.1 = (f32[144,2560]{1,0:T(8,128)S(1)}, s32[1]{0:T(128)}) custom-call(s32[6]{0:T(128)S(1)} %stack.67.where_ref, bf16[5,256,256]{2,1,0:T(8,128)(2,1)S(1)} %copy-done, bf16[5,256,256]{2,1,0:T(8,128)(2,1)S(1)} %collective-permute-done.1.other_ref, bf16[4,272,256]{2,1,0:T(8,128)(2,1)S(1)} %pad_maximum_fusion.refs_0_), custom_call_target="tpu_custom_call" | custom-call | flops 5368709120 | bytes 1048576 | tf_op jit(solution)/shard_map/own_plane/pallas_call | solution.py:278
  40.4 7.4 %planes.3 = (f32[144,2560]{1,0:T(8,128)S(1)}, s32[1]{0:T(128)}) custom-call(s32[1]{0:T(128)} %bitcast.9.count_ref, bf16[5,256,256]{2,1,0:T(8,128)(2,1)S(1)} %copy-done, bf16[5,256,256]{2,1,0:T(8,128)(2,1)S(1)} %collective-permute-done.1.other_ref, bf16[4,272,256]{2,1,0:T(8,128)(2,1)S(1)} %collective-permute-done.4.refs_0_, ...), custom_call_target="tpu_custom_call" | custom-call | flops 8053063680 | bytes 1048576 | tf_op jit(solution)/shard_map/planes/pallas_call | solution.py:313
  47.9 2.0 %collective-permute-start.10 = (bf16[4,272,256]{2,1,0:T(8,128)(2,1)S(1)}, bf16[4,272,256]{2,1,0:T(8,128)(2,1)S(1)}, u32[]{:S(2)}, u32[]{:S(2)}) collective-permute-start(bf16[4,272,256]{2,1,0:T(8,128)(2,1)S(1)} %collective-permute-done.9.refs_1_), channel_id=1, source_target_pairs={{0,224},{32,0},{64,32},{96,64},{128,96},{160,128},{192,160},{224,1... | collective-permute-start | bytes 1671176 | tf_op jit(solution)/shard_map/ppermute | solution.py:378
  49.9 7.2 %planes.4 = (f32[144,2560]{1,0:T(8,128)S(1)}, s32[1]{0:T(128)}) custom-call(s32[1]{0:T(128)} %bitcast.8.count_ref, bf16[5,256,256]{2,1,0:T(8,128)(2,1)S(1)} %copy-done, bf16[5,256,256]{2,1,0:T(8,128)(2,1)S(1)} %collective-permute-done.1.other_ref, bf16[4,272,256]{2,1,0:T(8,128)(2,1)S(1)} %collective-permute-done.5.refs_0_, ...), custom_call_target="tpu_custom_call" | custom-call | flops 8053063680 | bytes 1048576 | tf_op jit(solution)/shard_map/planes/pallas_call | solution.py:313
  58.7 7.2 %planes.5 = (f32[144,2560]{1,0:T(8,128)S(1)}, s32[1]{0:T(128)}) custom-call(s32[1]{0:T(128)} %bitcast.7.count_ref, bf16[5,256,256]{2,1,0:T(8,128)(2,1)S(1)} %copy-done, bf16[5,256,256]{2,1,0:T(8,128)(2,1)S(1)} %collective-permute-done.1.other_ref, bf16[4,272,256]{2,1,0:T(8,128)(2,1)S(1)} %collective-permute-done.6.refs_0_, ...), custom_call_target="tpu_custom_call" | custom-call | flops 8053063680 | bytes 1048576 | tf_op jit(solution)/shard_map/planes/pallas_call | solution.py:313
  67.6 1.9 %maximum_add_fusion.weights_1_.weights_0_ = bf16[1920,640]{1,0:T(8,128)(2,1)S(1)} fusion(bf16[640,640]{1,0:T(8,128)(2,1)} %collective-permute-done.19, bf16[640,640]{1,0:T(8,128)(2,1)} %collective-permute-done.18, bf16[640,640]{1,0:T(8,128)(2,1)S(1)} %collective-permute-done.17, bf16[]{:T(256)} %bitcast.16), kind=kLoop, calls=%fused_computation | loop fusion | flops 9830400 | bytes 4915202 | tf_op jit(solution)/shard_map/add | solution.py:445
  69.5 20.5 %collective-permute-start.20 = (bf16[1920,640]{1,0:T(8,128)(2,1)S(1)}, bf16[1920,640]{1,0:T(8,128)(2,1)}, u32[]{:S(2)}, u32[]{:S(2)}) collective-permute-start(bf16[1920,640]{1,0:T(8,128)(2,1)S(1)} %maximum_add_fusion.weights_1_.weights_0_), channel_id=1, source_target_pairs={{0,4},{4,0},{1,5},{5,1},{2,6},{6,2},{3,7},{7,3},{8,12},{12,8},{9,1... | collective-permute-start | bytes 7372808 | tf_op jit(solution)/shard_map/ppermute | solution.py:378
  90.0 2.0 %collective-permute-start.11 = (bf16[2,272,256]{2,1,0:T(8,128)(2,1)S(1)}, bf16[2,272,256]{2,1,0:T(8,128)(2,1)}, u32[]{:S(2)}, u32[]{:S(2)}) collective-permute-start(bf16[2,272,256]{2,1,0:T(8,128)(2,1)S(1)} %slice.9.refs_4_), channel_id=1, source_target_pairs={{0,224},{32,0},{64,32},{96,64},{128,96},{160,128},{192,160},{224,1... | collective-permute-start | bytes 835592 | tf_op jit(solution)/shard_map/ppermute | solution.py:378
  92.0 6.6 %collective-permute-done.7.refs_0_ = bf16[2,272,256]{2,1,0:T(8,128)(2,1)S(1)} collective-permute-done((bf16[2,272,256]{2,1,0:T(8,128)(2,1)S(1)}, bf16[2,272,256]{2,1,0:T(8,128)(2,1)S(1)}, u32[]{:S(2)}, u32[]{:S(2)}) %collective-permute-start.7) | collective-permute-done | bytes 278560 | tf_op jit(solution)/shard_map/ppermute | solution.py:378
  103.6 4.5 %last_planes.1 = (f32[5,136,256]{2,1,0:T(8,128)S(1)}, bf16[5,144,256]{2,1,0:T(8,128)(2,1)S(1)}) custom-call(s32[1]{0:T(128)} %bitcast.1.count_ref, bf16[5,256,256]{2,1,0:T(8,128)(2,1)S(1)} %copy-done.1, bf16[5,256,256]{2,1,0:T(8,128)(2,1)S(1)} %copy-done.3, bf16[2,272,256]{2,1,0:T(8,128)(2,1)S(1)} %collective-permute-done.7.refs_0_, ...), custom_call_target="tpu_custom_call" | custom-call | flops 4026531840 | bytes 1048576 | tf_op jit(solution)/shard_map/last_planes/pallas_call | solution.py:313
  108.2 1.7 %collective-permute-done.12.came_ref = bf16[5,144,256]{2,1,0:T(8,128)(2,1)S(1)} collective-permute-done((bf16[5,144,256]{2,1,0:T(8,128)(2,1)S(1)}, bf16[5,144,256]{2,1,0:T(8,128)(2,1)S(1)}, u32[]{:S(2)}, u32[]{:S(2)}) %collective-permute-start.12) | collective-permute-done | bytes 368672 | tf_op jit(solution)/shard_map/ppermute | solution.py:378
  111.7 1.7 %collective-permute-start.16 = (bf16[128,640]{1,0:T(8,128)(2,1)S(1)}, bf16[128,640]{1,0:T(8,128)(2,1)S(1)}, u32[]{:S(2)}, u32[]{:S(2)}) collective-permute-start(bf16[128,640]{1,0:T(8,128)(2,1)S(1)} %get-tuple-element.23.own_1_), channel_id=1, source_target_pairs={{0,3},{1,0},{2,1},{3,2},{4,7},{5,4},{6,5},{7,6},{8,11},{9,8},{10,9... | collective-permute-start | bytes 491528 | tf_op jit(solution)/shard_map/ppermute | solution.py:378
  113.8 2.9 %collective-permute-start.15 = (bf16[128,640]{1,0:T(8,128)(2,1)S(1)}, bf16[128,640]{1,0:T(8,128)(2,1)S(1)}, u32[]{:S(2)}, u32[]{:S(2)}) collective-permute-start(bf16[128,640]{1,0:T(8,128)(2,1)S(1)} %get-tuple-element.22.own_0_), channel_id=1, source_target_pairs={{0,3},{1,0},{2,1},{3,2},{4,7},{5,4},{6,5},{7,6},{8,11},{9,8},{10,9... | collective-permute-start | bytes 491528 | tf_op jit(solution)/shard_map/ppermute | solution.py:378
  116.6 1.8 %collective-permute-done.13.below_0_ = bf16[128,640]{1,0:T(8,128)(2,1)S(1)} collective-permute-done((bf16[128,640]{1,0:T(8,128)(2,1)S(1)}, bf16[128,640]{1,0:T(8,128)(2,1)S(1)}, u32[]{:S(2)}, u32[]{:S(2)}) %collective-permute-start.13) | collective-permute-done | bytes 163872 | tf_op jit(solution)/shard_map/ppermute | solution.py:378
  118.8 2.8 %collective-permute-start.22 = (bf16[128,640]{1,0:T(8,128)(2,1)S(1)}, bf16[128,640]{1,0:T(8,128)(2,1)S(1)}, u32[]{:S(2)}, u32[]{:S(2)}) collective-permute-start(bf16[128,640]{1,0:T(8,128)(2,1)S(1)} %collective-permute-done.16.above_1_), channel_id=1, source_target_pairs={{0,3},{1,0},{2,1},{3,2},{4,7},{5,4},{6,5},{7,6},{8,11},{9,8},{10,9... | collective-permute-start | bytes 491528 | tf_op jit(solution)/shard_map/ppermute | solution.py:378
  123.2 3.4 %project_near.1.near_ref = f32[256,1280]{1,0:T(8,128)S(1)} custom-call(s32[1]{0:T(128)} %bitcast.core_ref, bf16[128,640]{1,0:T(8,128)(2,1)S(1)} %get-tuple-element.22.own_0_, bf16[128,640]{1,0:T(8,128)(2,1)S(1)} %get-tuple-element.23.own_1_, bf16[128,640]{1,0:T(8,128)(2,1)S(1)} %collective-permute-done.13.below_0_, ...), custom_call_target="tpu_custom_call" | custom-call | tf_op jit(solution)/shard_map/project_near/pallas_call | solution.py:356
  126.7 3.3 %project_far.1 = bf16[256,1280]{1,0:T(8,128)(2,1)} custom-call(s32[1]{0:T(128)} %bitcast.core_ref, f32[256,1280]{1,0:T(8,128)S(1)} %project_near.1.near_ref, bf16[128,640]{1,0:T(8,128)(2,1)S(1)} %collective-permute-done.21.pair_0_, bf16[128,640]{1,0:T(8,128)(2,1)S(1)} %collective-permute-done.22.pair_1_, ...), custom_call_target="tpu_custom_call" | custom-call | tf_op jit(solution)/shard_map/project_far/pallas_call | solution.py:367
  (55 shorter events, 24.1 us)
Async XLA Ops:
  1.6 9.0 %collective-permute-start = (bf16[272,256]{1,0:T(8,128)(2,1)}, bf16[272,256]{1,0:T(8,128)(2,1)S(1)}, u32[]{:S(2)}, u32[]{:S(2)}) collective-permute-start(bf16[272,256]{1,0:T(8,128)(2,1)} %prepare_keys.1), channel_id=1, source_target_pairs={{0,24},{8,0},{16,8},{24,16},{1,25},{9,1},{17,9},{25,17},{2,26},{10... | collective-permute-start | bytes 417800 | tf_op jit(solution)/shard_map/ppermute | solution.py:378
  4.4 9.2 %collective-permute-start.3 = (bf16[272,256]{1,0:T(8,128)(2,1)}, bf16[272,256]{1,0:T(8,128)(2,1)S(1)}, u32[]{:S(2)}, u32[]{:S(2)}) collective-permute-start(bf16[272,256]{1,0:T(8,128)(2,1)} %prepare_keys.1), channel_id=1, source_target_pairs={{0,16},{8,24},{16,0},{24,8},{1,17},{9,25},{17,1},{25,9},{2,18},{10... | collective-permute-start | bytes 417800 | tf_op jit(solution)/shard_map/ppermute | solution.py:378
  5.2 9.0 %collective-permute-start.2 = (bf16[272,256]{1,0:T(8,128)(2,1)}, bf16[272,256]{1,0:T(8,128)(2,1)S(1)}, u32[]{:S(2)}, u32[]{:S(2)}) collective-permute-start(bf16[272,256]{1,0:T(8,128)(2,1)} %prepare_keys.1), channel_id=1, source_target_pairs={{0,8},{8,16},{16,24},{24,0},{1,9},{9,17},{17,25},{25,1},{2,10},{10... | collective-permute-start | bytes 417800 | tf_op jit(solution)/shard_map/ppermute | solution.py:378
  13.4 19.4 %collective-permute-start.1 = (bf16[5,256,256]{2,1,0:T(8,128)(2,1)}, bf16[5,256,256]{2,1,0:T(8,128)(2,1)S(1)}, u32[]{:S(2)}, u32[]{:S(2)}) collective-permute-start(bf16[5,256,256]{2,1,0:T(8,128)(2,1)} %get-tuple-element.15.mine_ref), channel_id=1, source_target_pairs={{0,4},{4,0},{1,5},{5,1},{2,6},{6,2},{3,7},{7,3},{8,12},{12,8},{9,1... | collective-permute-start | bytes 1966088 | tf_op jit(solution)/shard_map/ppermute | solution.py:378
  15.3 14.5 %collective-permute-start.4 = (bf16[4,272,256]{2,1,0:T(8,128)(2,1)S(1)}, bf16[4,272,256]{2,1,0:T(8,128)(2,1)S(1)}, u32[]{:S(2)}, u32[]{:S(2)}) collective-permute-start(bf16[4,272,256]{2,1,0:T(8,128)(2,1)S(1)} %pad_maximum_fusion.refs_0_), channel_id=1, source_target_pairs={{0,32},{32,64},{64,96},{96,128},{128,160},{160,192},{192,224},{224... | collective-permute-start | bytes 1671176 | tf_op jit(solution)/shard_map/ppermute | solution.py:378
  15.4 16.0 %collective-permute-start.8 = (bf16[4,272,256]{2,1,0:T(8,128)(2,1)S(1)}, bf16[4,272,256]{2,1,0:T(8,128)(2,1)S(1)}, u32[]{:S(2)}, u32[]{:S(2)}) collective-permute-start(bf16[4,272,256]{2,1,0:T(8,128)(2,1)S(1)} %pad_maximum_fusion.refs_0_), channel_id=1, source_target_pairs={{0,224},{32,0},{64,32},{96,64},{128,96},{160,128},{192,160},{224,1... | collective-permute-start | bytes 1671176 | tf_op jit(solution)/shard_map/ppermute | solution.py:378
  20.6 47.0 %collective-permute-start.19 = (bf16[640,640]{1,0:T(8,128)(2,1)}, bf16[640,640]{1,0:T(8,128)(2,1)}, u32[]{:S(2)}, u32[]{:S(2)}) collective-permute-start(bf16[640,640]{1,0:T(8,128)(2,1)} %get-tuple-element.26), channel_id=1, source_target_pairs={{0,2},{1,3},{2,0},{3,1},{4,6},{5,7},{6,4},{7,5},{8,10},{9,11},{10,... | collective-permute-start | bytes 2457608 | tf_op jit(solution)/shard_map/ppermute | solution.py:378
  23.8 43.8 %collective-permute-start.18 = (bf16[640,640]{1,0:T(8,128)(2,1)}, bf16[640,640]{1,0:T(8,128)(2,1)}, u32[]{:S(2)}, u32[]{:S(2)}) collective-permute-start(bf16[640,640]{1,0:T(8,128)(2,1)} %get-tuple-element.27), channel_id=1, source_target_pairs={{0,3},{1,0},{2,1},{3,2},{4,7},{5,4},{6,5},{7,6},{8,11},{9,8},{10,9... | collective-permute-start | bytes 2457608 | tf_op jit(solution)/shard_map/ppermute | solution.py:378
  29.8 37.8 %collective-permute-start.17 = (bf16[640,640]{1,0:T(8,128)(2,1)}, bf16[640,640]{1,0:T(8,128)(2,1)S(1)}, u32[]{:S(2)}, u32[]{:S(2)}) collective-permute-start(bf16[640,640]{1,0:T(8,128)(2,1)} %get-tuple-element.25), channel_id=1, source_target_pairs={{0,1},{1,2},{2,3},{3,0},{4,5},{5,6},{6,7},{7,4},{8,9},{9,10},{10,1... | collective-permute-start | bytes 2457608 | tf_op jit(solution)/shard_map/ppermute | solution.py:378
  31.4 16.4 %collective-permute-start.5 = (bf16[4,272,256]{2,1,0:T(8,128)(2,1)S(1)}, bf16[4,272,256]{2,1,0:T(8,128)(2,1)S(1)}, u32[]{:S(2)}, u32[]{:S(2)}) collective-permute-start(bf16[4,272,256]{2,1,0:T(8,128)(2,1)S(1)} %collective-permute-done.4.refs_0_), channel_id=1, source_target_pairs={{0,32},{32,64},{64,96},{96,128},{128,160},{160,192},{192,224},{224... | collective-permute-start | bytes 1671176 | tf_op jit(solution)/shard_map/ppermute | solution.py:378
  32.9 25.8 %copy-start.2 = (bf16[5,256,256]{2,1,0:T(8,128)(2,1)}, bf16[5,256,256]{2,1,0:T(8,128)(2,1)S(1)}, u32[]{:S(2)}) copy-start(bf16[5,256,256]{2,1,0:T(8,128)(2,1)S(1)} %collective-permute-done.1.other_ref) | copy-start | bytes 1966084
  32.9 15.0 %collective-permute-start.9 = (bf16[4,272,256]{2,1,0:T(8,128)(2,1)S(1)}, bf16[4,272,256]{2,1,0:T(8,128)(2,1)S(1)}, u32[]{:S(2)}, u32[]{:S(2)}) collective-permute-start(bf16[4,272,256]{2,1,0:T(8,128)(2,1)S(1)} %collective-permute-done.8.refs_1_), channel_id=1, source_target_pairs={{0,224},{32,0},{64,32},{96,64},{128,96},{160,128},{192,160},{224,1... | collective-permute-start | bytes 1671176 | tf_op jit(solution)/shard_map/ppermute | solution.py:378
  47.8 9.6 %collective-permute-start.6 = (bf16[4,272,256]{2,1,0:T(8,128)(2,1)S(1)}, bf16[4,272,256]{2,1,0:T(8,128)(2,1)S(1)}, u32[]{:S(2)}, u32[]{:S(2)}) collective-permute-start(bf16[4,272,256]{2,1,0:T(8,128)(2,1)S(1)} %collective-permute-done.5.refs_0_), channel_id=1, source_target_pairs={{0,32},{32,64},{64,96},{96,128},{128,160},{160,192},{192,224},{224... | collective-permute-start | bytes 1671176 | tf_op jit(solution)/shard_map/ppermute | solution.py:378
  47.9 10.8 %collective-permute-start.10 = (bf16[4,272,256]{2,1,0:T(8,128)(2,1)S(1)}, bf16[4,272,256]{2,1,0:T(8,128)(2,1)S(1)}, u32[]{:S(2)}, u32[]{:S(2)}) collective-permute-start(bf16[4,272,256]{2,1,0:T(8,128)(2,1)S(1)} %collective-permute-done.9.refs_1_), channel_id=1, source_target_pairs={{0,224},{32,0},{64,32},{96,64},{128,96},{160,128},{192,160},{224,1... | collective-permute-start | bytes 1671176 | tf_op jit(solution)/shard_map/ppermute | solution.py:378
  69.5 53.7 %collective-permute-start.20 = (bf16[1920,640]{1,0:T(8,128)(2,1)S(1)}, bf16[1920,640]{1,0:T(8,128)(2,1)}, u32[]{:S(2)}, u32[]{:S(2)}) collective-permute-start(bf16[1920,640]{1,0:T(8,128)(2,1)S(1)} %maximum_add_fusion.weights_1_.weights_0_), channel_id=1, source_target_pairs={{0,4},{4,0},{1,5},{5,1},{2,6},{6,2},{3,7},{7,3},{8,12},{12,8},{9,1... | collective-permute-start | bytes 7372808 | tf_op jit(solution)/shard_map/ppermute | solution.py:378
  90.0 8.7 %collective-permute-start.7 = (bf16[2,272,256]{2,1,0:T(8,128)(2,1)S(1)}, bf16[2,272,256]{2,1,0:T(8,128)(2,1)S(1)}, u32[]{:S(2)}, u32[]{:S(2)}) collective-permute-start(bf16[2,272,256]{2,1,0:T(8,128)(2,1)S(1)} %slice.8.refs_3_), channel_id=1, source_target_pairs={{0,32},{32,64},{64,96},{96,128},{128,160},{160,192},{192,224},{224... | collective-permute-start | bytes 835592 | tf_op jit(solution)/shard_map/ppermute | solution.py:378
  90.0 10.1 %collective-permute-start.11 = (bf16[2,272,256]{2,1,0:T(8,128)(2,1)S(1)}, bf16[2,272,256]{2,1,0:T(8,128)(2,1)}, u32[]{:S(2)}, u32[]{:S(2)}) collective-permute-start(bf16[2,272,256]{2,1,0:T(8,128)(2,1)S(1)} %slice.9.refs_4_), channel_id=1, source_target_pairs={{0,224},{32,0},{64,32},{96,64},{128,96},{160,128},{192,160},{224,1... | collective-permute-start | bytes 835592 | tf_op jit(solution)/shard_map/ppermute | solution.py:378
  108.1 1.8 %collective-permute-start.12 = (bf16[5,144,256]{2,1,0:T(8,128)(2,1)S(1)}, bf16[5,144,256]{2,1,0:T(8,128)(2,1)S(1)}, u32[]{:S(2)}, u32[]{:S(2)}) collective-permute-start(bf16[5,144,256]{2,1,0:T(8,128)(2,1)S(1)} %get-tuple-element.21), channel_id=1, source_target_pairs={{0,4},{4,0},{1,5},{5,1},{2,6},{6,2},{3,7},{7,3},{8,12},{12,8},{9,1... | collective-permute-start | bytes 1105928 | tf_op jit(solution)/shard_map/ppermute | solution.py:378
  110.1 8.3 %collective-permute-start.13 = (bf16[128,640]{1,0:T(8,128)(2,1)S(1)}, bf16[128,640]{1,0:T(8,128)(2,1)S(1)}, u32[]{:S(2)}, u32[]{:S(2)}) collective-permute-start(bf16[128,640]{1,0:T(8,128)(2,1)S(1)} %get-tuple-element.22.own_0_), channel_id=1, source_target_pairs={{0,1},{1,2},{2,3},{3,0},{4,5},{5,6},{6,7},{7,4},{8,9},{9,10},{10,1... | collective-permute-start | bytes 491528 | tf_op jit(solution)/shard_map/ppermute | solution.py:378
  111.7 7.1 %collective-permute-start.16 = (bf16[128,640]{1,0:T(8,128)(2,1)S(1)}, bf16[128,640]{1,0:T(8,128)(2,1)S(1)}, u32[]{:S(2)}, u32[]{:S(2)}) collective-permute-start(bf16[128,640]{1,0:T(8,128)(2,1)S(1)} %get-tuple-element.23.own_1_), channel_id=1, source_target_pairs={{0,3},{1,0},{2,1},{3,2},{4,7},{5,4},{6,5},{7,6},{8,11},{9,8},{10,9... | collective-permute-start | bytes 491528 | tf_op jit(solution)/shard_map/ppermute | solution.py:378
  113.4 9.8 %collective-permute-start.14 = (bf16[128,640]{1,0:T(8,128)(2,1)S(1)}, bf16[128,640]{1,0:T(8,128)(2,1)S(1)}, u32[]{:S(2)}, u32[]{:S(2)}) collective-permute-start(bf16[128,640]{1,0:T(8,128)(2,1)S(1)} %get-tuple-element.23.own_1_), channel_id=1, source_target_pairs={{0,1},{1,2},{2,3},{3,0},{4,5},{5,6},{6,7},{7,4},{8,9},{9,10},{10,1... | collective-permute-start | bytes 491528 | tf_op jit(solution)/shard_map/ppermute | solution.py:378
  113.8 9.4 %collective-permute-start.15 = (bf16[128,640]{1,0:T(8,128)(2,1)S(1)}, bf16[128,640]{1,0:T(8,128)(2,1)S(1)}, u32[]{:S(2)}, u32[]{:S(2)}) collective-permute-start(bf16[128,640]{1,0:T(8,128)(2,1)S(1)} %get-tuple-element.22.own_0_), channel_id=1, source_target_pairs={{0,3},{1,0},{2,1},{3,2},{4,7},{5,4},{6,5},{7,6},{8,11},{9,8},{10,9... | collective-permute-start | bytes 491528 | tf_op jit(solution)/shard_map/ppermute | solution.py:378
  118.4 8.3 %collective-permute-start.21 = (bf16[128,640]{1,0:T(8,128)(2,1)S(1)}, bf16[128,640]{1,0:T(8,128)(2,1)S(1)}, u32[]{:S(2)}, u32[]{:S(2)}) collective-permute-start(bf16[128,640]{1,0:T(8,128)(2,1)S(1)} %collective-permute-done.13.below_0_), channel_id=1, source_target_pairs={{0,1},{1,2},{2,3},{3,0},{4,5},{5,6},{6,7},{7,4},{8,9},{9,10},{10,1... | collective-permute-start | bytes 491528 | tf_op jit(solution)/shard_map/ppermute | solution.py:378
  118.8 7.9 %collective-permute-start.22 = (bf16[128,640]{1,0:T(8,128)(2,1)S(1)}, bf16[128,640]{1,0:T(8,128)(2,1)S(1)}, u32[]{:S(2)}, u32[]{:S(2)}) collective-permute-start(bf16[128,640]{1,0:T(8,128)(2,1)S(1)} %collective-permute-done.16.above_1_), channel_id=1, source_target_pairs={{0,3},{1,0},{2,1},{3,2},{4,7},{5,4},{6,5},{7,6},{8,11},{9,8},{10,9... | collective-permute-start | bytes 491528 | tf_op jit(solution)/shard_map/ppermute | solution.py:378
  (6 other events, 21.4 us)
